TPU v7x, 128 devices: a whole 4x4x4 slice. The times are simulated.
128 devices in a mesh: sub: 2 (over x_hi), row: 8 (over y, core), col: 8 (over x_lo, z).
Axes of the slice: x: 4 (x_hi: 2, x_lo: 2; x = x_hi * 2 + x_lo), y: 4, z: 4, core: 2. Of those that a mesh axis runs over, the one named last changes fastest.
Arguments:
- child_fronts: float32 [2, 8192, 8192], P('sub', 'row', 'col'), as said below
- child_map: int32 [2, 56], replicated, may hold values from 0 to 95, as said below
- parent_front: float32 [12288, 12288], P(('sub', 'row'), 'col'), as said below
Outputs:
- child_factor: float32 [2, 8192, 1024], P('sub', 'row', 'col')
- parent_factor: float32 [12288, 1024], P(('sub', 'row'), 'col')
- parent_update: float32 [12288, 12288], P(('sub', 'row'), 'col')
Inputs may be any that keep to these rules, and one draw needn't show every extreme that they name: The kept blocks of child c are numbered a = 0 .. 55 in increasing order; child_map[c, a] is the parent block that receives kept block a. A child's entries are distinct. Within each run of 7 entries of one child that starts at a multiple of that length, the values child_map // 12 are distinct; for children 2h and 2h + 1 and the same run, the 2 * (7) values child_map // 6 are distinct. `child_fronts`: each front is symmetric with smallest eigenvalue above 0.05. `parent_front`: symmetric with smallest eigenvalue above 0.05.
All inputs are finite; a program needn't handle non-finite values.
Results may differ from a plain program's by a relative error of at most 0.0003.
Values sent between devices are 32-bit elements; how exact they have to be, the bound alone decides.
No kernel may reach another device: no remote copies, remote signals or barrier semaphores. Data moves between devices by JAX's collectives and lax.ppermute only.
A program may use at most 192 MiB of HBM per device.

v0:
```python
import jax
import jax.numpy as jnp
from jax import lax
from jax.sharding import PartitionSpec as P

TILE = 128
STEPS = 8
CBLK = 64
PBLK = 96


HIGH = lax.Precision.HIGHEST


def pivot_tiles(array, axis, every, tile):
    count = array.shape[axis] // tile
    shape = array.shape[:axis] + (count // every, every, tile) + array.shape[axis + 1 :]
    picked = lax.index_in_dim(array.reshape(shape), 0, axis + 1, keepdims=False)
    return picked.reshape(array.shape[:axis] + (count // every * tile,) + array.shape[axis + 1 :])


def solve_panel(panel, lower):
    solved = jax.scipy.linalg.solve_triangular(lower, jnp.swapaxes(panel, -1, -2), lower=True)
    return jnp.swapaxes(solved, -1, -2)


def place_pivots(panel, lower, first_tile, spacing, tile):
    count = panel.shape[-2] // tile
    glob = first_tile + jnp.arange(count, dtype=jnp.int32)
    pivot = jnp.repeat(glob % spacing == 0, tile)
    which = jnp.clip(glob // spacing, 0, STEPS - 1)
    lower_tiles = lower.reshape(lower.shape[:-2] + (STEPS, tile, lower.shape[-1]))
    placed = jnp.take(lower_tiles, which, axis=-3).reshape(panel.shape)
    return jnp.where(pivot[:, None], placed, panel)


def children_gathered(fronts, row_id, col_id, spacing, tile):
    tiles_row = fronts.shape[1] // tile
    tiles_col = fronts.shape[2] // tile
    per_col = STEPS // lax.axis_size("col")
    columns = lax.all_gather(pivot_tiles(fronts, 2, spacing, tile), "col", axis=2, tiled=True)
    rows_piece = pivot_tiles(fronts, 1, spacing, tile)
    block_piece = pivot_tiles(columns, 1, spacing, tile)
    panel_rows, block = (
        lax.all_gather(rows_piece, "row", axis=1, tiled=True),
        lax.all_gather(block_piece, "row", axis=1, tiled=True),
    )
    lower = jnp.linalg.cholesky(block)
    left = place_pivots(solve_panel(columns, lower), lower, row_id * tiles_row, spacing, tile)
    right = place_pivots(
        solve_panel(jnp.swapaxes(panel_rows, 1, 2), lower), lower, col_id * tiles_col, spacing, tile
    )
    fronts = fronts - jnp.einsum("cni,cmi->cnm", left, right, precision=HIGH)
    factor = lax.dynamic_slice_in_dim(left, col_id * (per_col * tile), per_col * tile, 2)
    return (fronts, factor)


def parent_gathered(front, row_id, col_id, spacing, tile):
    tiles_row = front.shape[0] // tile
    tiles_col = front.shape[1] // tile
    per_col = STEPS // lax.axis_size("col")
    columns = lax.all_gather(pivot_tiles(front, 1, spacing, tile), "col", axis=1, tiled=True)
    local_tile = jnp.arange(STEPS, dtype=jnp.int32) * spacing - row_id * tiles_row
    present = (local_tile >= 0) & (local_tile < tiles_row)
    begins = jnp.clip(local_tile, 0, tiles_row - 1) * tile

    def pick(source, begin):
        return lax.dynamic_slice_in_dim(source, begin, tile, 0)

    rows_piece = jax.vmap(pick, (None, 0))(front, begins)
    block_piece = jax.vmap(pick, (None, 0))(columns, begins)
    rows_piece = jnp.where(present[:, None, None], rows_piece, 0.0).reshape(
        STEPS * tile, front.shape[1]
    )
    block_piece = jnp.where(present[:, None, None], block_piece, 0.0).reshape(
        STEPS * tile, STEPS * tile
    )
    panel_rows, block = lax.psum((rows_piece, block_piece), ("sub", "row"))
    lower = jnp.linalg.cholesky(block)
    left = place_pivots(solve_panel(columns, lower), lower, row_id * tiles_row, spacing, tile)
    right = place_pivots(solve_panel(panel_rows.T, lower), lower, col_id * tiles_col, spacing, tile)
    front = front - jnp.dot(left, right.T, precision=HIGH)
    factor = lax.dynamic_slice_in_dim(left, col_id * (per_col * tile), per_col * tile, 1)
    return (front, factor)


def assemble(fronts, child_map, parent_front, sub_id, row_id, col_id, spacing, tile):
    n_sub = lax.axis_size("sub")
    n_row = lax.axis_size("row")
    n_col = lax.axis_size("col")
    n_dev = n_sub * n_row * n_col
    count = fronts.shape[0]
    tiles_row = fronts.shape[1] // tile
    tiles_col = fronts.shape[2] // tile
    kept_row = tiles_row // spacing * (spacing - 1)
    kept_col = tiles_col // spacing * (spacing - 1)
    parent_rows = parent_front.shape[0] // tile
    parent_cols = parent_front.shape[1] // tile
    parent_spacing = PBLK // STEPS
    capacity = (
        tiles_row
        // spacing
        * (tiles_col // spacing)
        * max(1, parent_rows // (parent_spacing // 2))
        * max(1, parent_cols // parent_spacing)
    )
    blocks = fronts.reshape(
        count, tiles_row // spacing, spacing, tile, tiles_col // spacing, spacing, tile
    )
    blocks = blocks[:, :, 1:, :, :, 1:, :].transpose(0, 1, 2, 4, 5, 3, 6)
    blocks = blocks.reshape(count * kept_row * kept_col, tile, tile)
    rows_map = child_map.reshape(n_sub, count, n_row, kept_row)
    cols_map = child_map.reshape(n_sub, count, n_col, kept_col)
    my_rows = rows_map[sub_id][:, row_id]
    my_cols = cols_map[sub_id][:, col_id]
    target_dev = my_rows[:, :, None] // parent_rows * n_col + my_cols[:, None, :] // parent_cols
    target_dev = target_dev.reshape(-1)
    n_sent = target_dev.shape[0]
    same = target_dev[:, None] == target_dev[None, :]
    earlier = (
        jnp.arange(n_sent, dtype=jnp.int32)[None, :] < jnp.arange(n_sent, dtype=jnp.int32)[:, None]
    )
    rank = jnp.sum((same & earlier).astype(jnp.int32), axis=1)
    outbox = jnp.zeros((n_dev, capacity, tile, tile), jnp.float32).at[target_dev, rank].set(blocks)
    inbox = lax.all_to_all(outbox, ("sub", "row", "col"), split_axis=0, concat_axis=0, tiled=True)
    inbox = inbox.reshape(n_dev * capacity, tile, tile)
    here_row = lax.axis_index(("sub", "row"))
    rows_src = rows_map.transpose(0, 2, 1, 3)
    cols_src = cols_map.transpose(0, 2, 1, 3)
    row_hit = rows_src // parent_rows == here_row
    col_hit = cols_src // parent_cols == col_id
    hit = row_hit[:, :, None, :, :, None] & col_hit[:, None, :, :, None, :]
    spot = (rows_src - here_row * parent_rows)[:, :, None, :, :, None] * parent_cols + (
        cols_src - col_id * parent_cols
    )[:, None, :, :, None, :]
    hit = hit.reshape(n_dev, -1)
    spot = spot.reshape(n_dev, -1)
    order = jnp.cumsum(hit.astype(jnp.int32), axis=1) - 1
    slots = jnp.arange(capacity, dtype=jnp.int32)
    match = hit[:, None, :] & (order[:, None, :] == slots[None, :, None])
    landing = jnp.sum(jnp.where(match, spot[:, None, :], 0), axis=2)
    valid = jnp.any(match, axis=2)
    landing = jnp.where(valid, landing, parent_rows * parent_cols).reshape(-1)
    parent_tiles = parent_front.reshape(parent_rows, tile, parent_cols, tile).transpose(0, 2, 1, 3)
    parent_tiles = parent_tiles.reshape(parent_rows * parent_cols, tile, tile)
    parent_tiles = parent_tiles.at[landing].add(inbox, mode="drop")
    parent_tiles = parent_tiles.reshape(parent_rows, parent_cols, tile, tile).transpose(0, 2, 1, 3)
    return parent_tiles.reshape(parent_front.shape)


def local(child_fronts, child_map, parent_front):
    tile = TILE
    sub_id = lax.axis_index("sub")
    row_id = lax.axis_index("row")
    col_id = lax.axis_index("col")
    fronts, child_factor = children_gathered(child_fronts, row_id, col_id, CBLK // STEPS, tile)
    assembled = assemble(
        fronts, child_map, parent_front, sub_id, row_id, col_id, CBLK // STEPS, tile
    )
    parent_row = lax.axis_index(("sub", "row"))
    spacing = PBLK // STEPS
    front, parent_factor = parent_gathered(assembled, parent_row, col_id, spacing, tile)
    tiles_row = front.shape[0] // tile
    tiles_col = front.shape[1] // tile
    row_glob = parent_row * tiles_row + jnp.arange(tiles_row, dtype=jnp.int32)
    col_glob = col_id * tiles_col + jnp.arange(tiles_col, dtype=jnp.int32)
    row_keep = jnp.repeat(row_glob % spacing != 0, tile)
    col_keep = jnp.repeat(col_glob % spacing != 0, tile)
    parent_update = jnp.where(row_keep[:, None] & col_keep[None, :], front, 0.0)
    return (child_factor, parent_factor, parent_update)


def solution(mesh):
    in_specs = (P("sub", "row", "col"), P(), P(("sub", "row"), "col"))
    out_specs = (P("sub", "row", "col"), P(("sub", "row"), "col"), P(("sub", "row"), "col"))
    return jax.shard_map(local, mesh=mesh, in_specs=in_specs, out_specs=out_specs, check_vma=False)
```

profile of v0, /device:TPU:1, one launch (start us, length us, event | category | flops | bytes accessed | tf_op | source)
XLA Modules:
  0.0 1408.4 jit_solution(7930297600783837057)
XLA Ops:
  14.5 56.1 %all-gather.9.cloned.1.call-done = f32[1,1024,1,1,1024]{1,4,3,2,0:T(8,128)} async-done(((f32[1,1024,1,1,128]{1,4,3,2,0:T(8,128)}), f32[1,1024,1,1,1024]{1,4,3,2,0:T(8,128)}) %all-gather.9.cloned.1.call-update) | async-done | bytes 4194320 | tf_op jit(solution)/shard_map/all_gather | solution.py:41
  81.0 32.4 %all-gather.11.cloned.1.call-done = f32[1,1,1,1024,1024]{3,4,2,1,0:T(8,128)} async-done(((f32[1,1,1,128,1024]{3,4,2,1,0:T(8,128)}), f32[1,1,1,1024,1024]{3,4,2,1,0:T(8,128)}) %all-gather.11.cloned.1.call-update) | async-done | bytes 4194320 | tf_op jit(solution)/shard_map/all_gather | solution.py:46
  125.1 11.7 custom-call.136
  153.1 12.0 custom-call.138
  178.9 11.7 custom-call.140
  204.6 11.9 custom-call.142
  230.4 11.7 custom-call.144
  242.7 10.2 custom-call.145
  256.2 11.7 custom-call.146
  281.3 11.7 custom-call.148
  306.1 11.7 custom-call.150
  350.2 23.2 %while.10 = (s32[]{:T(128)}, f32[1024,1024]{1,0:T(8,128)}, s32[8,2]{0,1:T(2,128)S(1)}, f32[8,128,128]{2,1,0:T(8,128)S(1)}, s32[]{:T(128)}) while((s32[]{:T(128)}, f32[1024,1024]{1,0:T(8,128)}, s32[8,2]{0,1:T(2,128)S(1)}, f32[8,128,128]{2,1,0:T(8,128)S(1)}, s32[]{:T(128)}) %tuple.202), condition=%wide.while_cond, body=%wide.while_body.sunk | while | flops 2 | bytes 131189 | solution.py:23
  373.4 78.6 %custom-call.160 = f32[8,128,128]{1,2,0:T(8,128)S(1)} custom-call(f32[8,128,128]{2,1,0:T(8,128)S(1)} %get-tuple-element.43), custom_call_target="InvertDiagBlocksLowerTriangular" | custom-call | tf_op jit(solution)/shard_map/jit(_solve_triangular)/triangular_solve | solution.py:23
  526.0 14.9 %fusion.7 = f32[128,8,8,128]{3,1,2,0:T(8,128)S(1)} fusion(f32[1,1024,1024]{2,1,0:T(8,128)S(1)} %copy-done.2, f32[1,1024,1024]{1,2,0:T(8,128)S(1)} %copy-done.4, f32[1024,1024]{1,0:T(8,128)S(1)} %convolution_dynamic-update-slice_fusion.1, pred[1024]{0:T(1024)(128)(4,1)S(1)} %broadcast_bitcast_fusion.4, f32[1,1024,1024]{1,2,0:T(8,128)S(1)} %bitcast_select_fusion.4), kind=kOutput, calls=%fused_computation.30 | convolution fusion | flops 12886999040 | bytes 20972544 | tf_op jit(solution)/shard_map/cni,cmi->cnm/dot_general | solution.py:53
  547.1 10.0 scatter_fusion
  581.6 87.5 %all-to-all-done = f32[128,1,128,128]{3,2,1,0:T(8,128)} async-done(((f32[128,1,128,128]{3,2,1,0:T(8,128)}), f32[128,1,128,128]{3,2,1,0:T(8,128)}, u32[]{:S(2)}, u32[]{:S(2)}) %all-to-all-start) | async-done | bytes 8388640 | tf_op jit(solution)/shard_map/all_to_all | solution.py:125
  669.1 25.5 %scatter_fusion.1 = f32[72,128,128]{2,1,0:T(8,128)} fusion(f32[72,128,128]{2,1,0:T(8,128)} %bitcast.614, s32[128]{0:T(128)S(1)} %fusion.214, f32[128,128,128]{2,1,0:T(8,128)} %bitcast.122), kind=kCustom, calls=%fused_computation.5 | custom fusion | flops 2097152 | bytes 25166336 | tf_op jit(solution)/shard_map/scatter-add | solution.py:146
  708.3 27.0 %while.9 = (s32[]{:T(128)}, f32[768,1536]{1,0:T(8,128)}, s32[8,2]{0,1:T(2,128)S(1)}, f32[8,128,1536]{2,1,0:T(8,128)}, s32[]{:T(128)}) while((s32[]{:T(128)}, f32[768,1536]{1,0:T(8,128)}, s32[8,2]{0,1:T(2,128)S(1)}, f32[8,128,1536]{2,1,0:T(8,128)}, s32[]{:T(128)}) %tuple.225), condition=%wide.while_cond.3, body=%wide.while_body.3.sunk | while | flops 2 | bytes 1573477 | solution.py:68
  744.1 28.5 %while.7 = (s32[]{:T(128)}, f32[768,1024]{0,1:T(8,128)}, s32[8,2]{0,1:T(2,128)S(1)}, f32[8,128,1024]{2,1,0:T(8,128)}, s32[]{:T(128)}) while((s32[]{:T(128)}, f32[768,1024]{0,1:T(8,128)}, s32[8,2]{0,1:T(2,128)S(1)}, f32[8,128,1024]{2,1,0:T(8,128)}, s32[]{:T(128)}) %tuple.227), condition=%wide.while_cond.1, body=%wide.while_body.1.sunk | while | flops 2 | bytes 3145833 | solution.py:68
  787.3 168.1 %all-reduce.6.cloned.1.call-done = (f32[1024,1024]{0,1:T(8,128)}, f32[1024,1536]{1,0:T(8,128)}) async-done(((f32[1024,1024]{0,1:T(8,128)}, f32[1024,1536]{1,0:T(8,128)}), (f32[1024,1024]{0,1:T(8,128)}, f32[1024,1536]{1,0:T(8,128)})) %all-reduce.6.cloned.1.call-update) | async-done | bytes 10485776 | tf_op jit(solution)/shard_map/psum | solution.py:78
  967.4 11.7 cholesky.1011
  979.2 9.8 custom-call.151
  992.4 11.7 cholesky.1030
  1019.9 11.7 cholesky.1051
  1046.8 11.7 cholesky.1070
  1073.4 12.1 cholesky.1089
  1100.3 11.7 cholesky.1109
  1126.5 11.7 cholesky.1129
  1151.9 11.7 cholesky.1147
  1182.4 28.8 %while.8 = (s32[]{:T(128)}, f32[1024,1024]{0,1:T(8,128)}, s32[8,2]{0,1:T(2,128)S(1)}, f32[8,128,128]{2,1,0:T(8,128)}, s32[]{:T(128)}) while((s32[]{:T(128)}, f32[1024,1024]{0,1:T(8,128)}, s32[8,2]{0,1:T(2,128)S(1)}, f32[8,128,128]{2,1,0:T(8,128)}, s32[]{:T(128)}) %tuple.228), condition=%wide.while_cond.2, body=%wide.while_body.2.sunk | while | flops 2 | bytes 393329 | solution.py:23
  1211.2 80.4 %custom-call.158 = f32[8,128,128]{1,2,0:T(8,128)} custom-call(f32[8,128,128]{2,1,0:T(8,128)} %get-tuple-element.28), custom_call_target="InvertDiagBlocksLowerTriangular" | custom-call | tf_op jit(solution)/shard_map/jit(_solve_triangular)/triangular_solve | solution.py:23
  1381.3 20.1 %subtract_select_fusion = f32[768,1536]{1,0:T(8,128)} fusion(f32[768,1536]{1,0:T(8,128)} %get-tuple-element.488, f32[768,1024]{0,1:T(8,128)S(1)} %bitcast_select_fusion.10, f32[1024,1536]{1,0:T(8,128)} %convolution_dynamic-update-slice_fusion, f32[1536,1024]{0,1:T(8,128)} %copy.186, pred[1536]{0:T(1024)(128)(4,1)S(1)} %broadcast_bitcast_fusion, ...), kind=kOutput, calls=%fused_computation.20 | convolution fusion | flops 14502199296 | bytes 25171200 | tf_op jit(solution)/shard_map/dot_general | solution.py:82
  (446 shorter events, 600.8 us)
Async XLA Ops:
  7.2 63.5 %all-gather.9.cloned.1.call-start = ((), (), s32[]{:S(2)}) async-start(), calls=%async_computation.1 | async-start | bytes 4718592 | tf_op jit(solution)/shard_map/all_gather | solution.py:41
  14.5 98.9 %all-gather.11.cloned.1.call-start = ((), (), s32[]{:S(2)}) async-start(), calls=%async_computation.2 | async-start | bytes 4718592 | tf_op jit(solution)/shard_map/all_gather | solution.py:46
  76.0 4.2 copy-start.13
  78.1 417.9 %all-gather.13.cloned.1.call-start = ((), (), s32[]{:S(2)}) async-start(), calls=%async_computation.3 | async-start | bytes 4718592 | tf_op jit(solution)/shard_map/all_gather | solution.py:45
  123.1 2.0 copy-start.7
  467.7 5.9 copy-start.5
  496.0 4.3 copy-start.10
  514.9 6.3 copy-start.3
  521.3 3.5 copy-start.2
  521.3 4.7 copy-start.4
  526.0 14.9 %copy-start.1 = (f32[1,1024,1024]{1,2,0:T(8,128)}, f32[1,1024,1024]{1,2,0:T(8,128)S(1)}, u32[]{:S(2)}) copy-start(f32[1,1024,1024]{1,2,0:T(8,128)S(1)} %bitcast_select_fusion.4) | copy-start | bytes 12582916
  557.1 112.0 %all-to-all-start = ((f32[128,1,128,128]{3,2,1,0:T(8,128)}), f32[128,1,128,128]{3,2,1,0:T(8,128)}, u32[]{:S(2)}, u32[]{:S(2)}) async-start(f32[128,1,128,128]{3,2,1,0:T(8,128)} %bitcast.617), calls=%async_computation | async-start | bytes 16777216 | tf_op jit(solution)/shard_map/all_to_all | solution.py:125
  566.5 177.7 %all-gather.15.cloned.1.call-start = ((), (), s32[]{:S(2)}) async-start(), calls=%async_computation.4 | async-start | bytes 3538944 | tf_op jit(solution)/shard_map/all_gather | solution.py:62
  698.5 256.8 %all-reduce.6.cloned.1.call-start = ((), (), s32[]{:S(2)}) async-start(), calls=%async_computation.5 | async-start | bytes 20971520 | tf_op jit(solution)/shard_map/psum | solution.py:78
  965.3 2.0 copy-start.6
  1015.5 2.0 copy-start
  1174.7 116.9 %copy-start.8 = (f32[768,1024]{0,1:T(8,128)S(1)}, f32[768,1024]{0,1:T(8,128)}, u32[]{:S(2)}) copy-start(f32[768,1024]{0,1:T(8,128)} %get-tuple-element.499) | copy-start | bytes 9437188
  1291.6 5.8 copy-start.11
  1308.9 3.2 copy-start.9
  1329.5 5.2 copy-start.12
  1334.7 6.1 slice-start
  1336.6 4.2 slice-start.1
Sparse Core Ops, SparseCore 0:
  14.6 55.9 all-gather.8
  78.2 35.1 all-gather.10
  115.1 33.0 all-gather.12
  698.6 45.4 all-gather.14
  783.1 172.2 all-reduce.5
where the time goes:
time: 1420 us; the launch traced here: 1410 us
  other arithmetic  577 us (41%)
  waiting for transfers between devices  347 us (24%)
  local copies, waits for them, and re-layouts  250 us (18%)
  matrix products  199 us (14%)
  between operations  25.4 us (2%)
    another operation x5, other arithmetic, solve_panel(): jax.scipy.linalg.solve_triangular(lower, jnp.swapaxes(panel, -1, -2), low...  173 us
    another operation x30, other arithmetic, children_gathered(): lower = jnp.linalg.cholesky(block)  172 us
    another operation x31, other arithmetic, parent_gathered(): lower = jnp.linalg.cholesky(block)  169 us
    psum x1, waiting for transfers between devices, parent_gathered(): panel_rows, block = lax.psum((rows_piece, block_piece), ('sub', 'row'))  168 us
    another operation x60, matrix products, solve_panel(): jax.scipy.linalg.solve_triangular(lower, jnp.swapaxes(panel, -1, -2), low...  115 us
    all_to_all x1, waiting for transfers between devices, assemble(): lax.all_to_all(outbox, ('sub', 'row', 'col'), split_axis=0, concat_axis=0...  87.5 us
    all_gather x1, waiting for transfers between devices, children_gathered(): lax.all_gather(pivot_tiles(fronts, 2, spacing, tile), 'col', axis=2, tile...  56.1 us
    gather x64, local copies, waits for them, and re-layouts  55.4 us
  transfers between devices with their start and end apart: 6, of which 5 were waited for; matrix products, arithmetic and copies ran while one was open for 31% of the time, Pallas kernels for 0%

commit v1 on v0

v1 whole, which is shorter than its diff:
```python
import functools

import jax
import jax.numpy as jnp
from jax import lax
from jax.experimental import pallas as pl
from jax.experimental.pallas import tpu as pltpu
from jax.sharding import PartitionSpec as P

TILE = 128
STEPS = 8
CBLK = 64
PBLK = 96
ORDER = TILE * STEPS

SWAP = [(0, 1), (1, 0)]
GROUP = ("sub", "y")
COL = ("xlo", "z")
VMEM = pl.BlockSpec(memory_space=pltpu.VMEM)
SMEM = pl.BlockSpec(memory_space=pltpu.SMEM)


def split(x):
    high = x.astype(jnp.bfloat16)
    return high, (x - high.astype(jnp.float32)).astype(jnp.bfloat16)


def dot3(a, b, contract):
    dot = functools.partial(
        lax.dot_general, dimension_numbers=(contract, ((), ())), preferred_element_type=jnp.float32
    )
    return dot(a[0], b[0]) + (dot(a[0], b[1]) + dot(a[1], b[0]))


def factor_tile(s_ref, u_ref, x_ref):
    full = (8, TILE)
    lane = lax.broadcasted_iota(jnp.int32, full, 1)
    sub = lax.broadcasted_iota(jnp.int32, full, 0)
    for p in range(TILE // 8):
        j0 = 8 * p
        inside = (lane >= j0) & (lane < j0 + 8)
        panel = s_ref[j0 : j0 + 8, :]
        cols = [jnp.broadcast_to(panel[:, j0 + k : j0 + k + 1], full) for k in range(8)]
        c = [[jnp.broadcast_to(cols[m][k : k + 1, :], full) if m >= k else None for m in range(8)] for k in range(8)]
        low = [[None] * 8 for _ in range(8)]
        inv, root = [None] * 8, [None] * 8
        for k in range(8):
            root[k] = lax.rsqrt(c[k][k])
            inv[k] = root[k] * root[k]
            for m in range(k + 1, 8):
                low[m][k] = c[k][m] * inv[k]
            for m in range(k + 1, 8):
                for n in range(m, 8):
                    c[m][n] = c[m][n] - low[m][k] * c[k][n]
        e = []
        for k in range(8):
            row = jnp.broadcast_to(panel[k : k + 1, :], full)
            row = jnp.where(inside, jnp.where(lane == j0 + k, 1.0, 0.0), row)
            for m in range(k):
                row = row - low[k][m] * e[m]
            e.append(row)
        q = [None] * 8
        for k in reversed(range(8)):
            row = inv[k] * e[k]
            for m in range(k + 1, 8):
                row = row - low[m][k] * q[m]
            q[k] = row
        out = jnp.zeros(full, jnp.float32)
        diag = jnp.zeros(full, jnp.float32)
        for k in range(8):
            out = jnp.where(sub == k, e[k] * root[k], out)
            for m in range(k, 8):
                diag = jnp.where((sub == k) & (lane == j0 + m), c[k][m] * root[k], diag)
        x_ref[j0 : j0 + 8, :] = jnp.where(lane < j0 + 8, out, 0.0)
        u_ref[j0 : j0 + 8, :] = jnp.where(lane >= j0 + 8, out, diag)
        for i in range(p + 1, TILE // 8):
            old = s_ref[8 * i : 8 * i + 8, :]
            new = jnp.where(inside, 0.0, old)
            for k in range(8):
                new = new - jnp.broadcast_to(old[:, j0 + k : j0 + k + 1], full) * q[k]
            s_ref[8 * i : 8 * i + 8, :] = new


def factor_kernel(core_ref, own_ref, other_ref, u_ref, x_ref, w_ref, s_ref, uk_ref, xk_ref, row_ref):
    core = core_ref[0]
    groups, depth = own_ref.shape[1], own_ref.shape[2]
    pitch = ORDER // groups
    for ref, which in ((own_ref, core), (other_ref, 1 - core)):
        for g in range(groups):
            begin = pl.multiple_of(g * pitch + which * depth, depth)
            for c in range(STEPS):
                w_ref[pl.ds(begin, depth), c * TILE : (c + 1) * TILE] = ref[c, g]
    block = lax.broadcasted_iota(jnp.int32, (TILE, ORDER), 1) // TILE

    def step(k, carry):
        here = pl.ds(pl.multiple_of(k * TILE, TILE), TILE)
        s_ref[...] = w_ref[here, here]
        factor_tile(s_ref, uk_ref, xk_ref)
        row_ref[...] = dot3(split(xk_ref[...]), split(w_ref[here, :]), ((1,), (0,)))
        row_ref[:, here] = xk_ref[...]
        new = row_ref[...]
        x_ref[here, :] = jnp.where(block <= k, new, 0.0)
        u_ref[here, :] = jnp.where(block > k, new, 0.0)
        u_ref[here, here] = uk_ref[...]
        right = split(new)

        def trail(i, carry):
            at = pl.ds(pl.multiple_of(i * TILE, TILE), TILE)
            w_ref[at, here] = jnp.zeros((TILE, TILE), jnp.float32)
            w_ref[at, :] -= dot3(split(row_ref[:, at].T), right, ((1,), (0,)))
            return carry

        lax.fori_loop(k + 1, STEPS, trail, 0)
        return carry

    lax.fori_loop(0, STEPS, step, 0)


def factor(core, own, other):
    out = jax.ShapeDtypeStruct((ORDER, ORDER), jnp.float32)
    return pl.pallas_call(
        factor_kernel,
        out_shape=(out, out),
        in_specs=[SMEM, VMEM, VMEM],
        out_specs=(VMEM, VMEM),
        scratch_shapes=[pltpu.VMEM((ORDER, ORDER), jnp.float32)]
        + [pltpu.VMEM((TILE, TILE), jnp.float32)] * 3
        + [pltpu.VMEM((TILE, ORDER), jnp.float32)],
        compiler_params=pltpu.CompilerParams(vmem_limit_bytes=40 << 20),
        cost_estimate=pl.CostEstimate(flops=100_000_000_000, bytes_accessed=16 << 20, transcendentals=0),
        name="factor",
    )(core.reshape(1), own, other)


def solve_panels(col, cols_ref, x_ref, factor_ref, xs, cs, rs, ls, ts):
    wide = 2 * TILE
    xs[0][...], xs[1][...] = split(x_ref[...])
    for c in range(STEPS):
        at = slice(c * TILE, (c + 1) * TILE)
        cs[0][:, at], cs[1][:, at] = split(cols_ref[c])
    for k in range(STEPS // 2):
        depth = wide * (k + 1)
        at = slice(k * wide, depth)
        x_now = (xs[0][at, :depth], xs[1][at, :depth])
        left = dot3((cs[0][:, :depth], cs[1][:, :depth]), x_now, ((1,), (1,)))
        ls[0][:, at], ls[1][:, at] = split(left)
        for half in range(2):

            @pl.when(col == 2 * k + half)
            def _():
                factor_ref[...] = left[:, half * TILE : (half + 1) * TILE]

        def turn(n, carry):
            here = pl.ds(pl.multiple_of(n * wide, wide), wide)
            right = dot3(x_now, (rs[0][:depth, here], rs[1][:depth, here]), ((1,), (0,)))
            ts[0][at, here], ts[1][at, here] = split(right)
            return carry

        lax.fori_loop(0, rs[0].shape[1] // wide, turn, 0)


def child_kernel(where_ref, front_ref, cols_ref, rows_ref, x_ref, lower_ref, box_ref, factor_ref, *scratch):
    xs, cs, rs, ls, ts = (scratch[i : i + 2] for i in range(0, 10, 2))
    wide = 2 * TILE
    col = where_ref[0]
    rs[0][...], rs[1][...] = split(rows_ref[...])
    solve_panels(col, cols_ref, x_ref, factor_ref, xs, cs, rs, ls, ts)
    factor_ref[:TILE, :] = lower_ref[...]
    left = (ls[0][...], ls[1][...])

    def chunk(n, carry):
        here = pl.ds(pl.multiple_of(n * wide, wide), wide)
        schur = front_ref[:, here] - dot3(left, (ts[0][:, here], ts[1][:, here]), ((1,), (0,)))
        for half in range(2):
            b = 2 * n + half

            @pl.when(b > 0)
            def _():
                for a in range(1, STEPS):
                    slot = where_ref[a] * STEPS + where_ref[STEPS + b]
                    box_ref[slot] = schur[a * TILE : (a + 1) * TILE, half * TILE : (half + 1) * TILE]

        return carry

    lax.fori_loop(0, front_ref.shape[1] // wide, chunk, 0)


def panel_scratch(rows, cols):
    shapes = [(ORDER, ORDER), (rows, ORDER), (ORDER, cols), (rows, ORDER), (ORDER, cols)]
    return [pltpu.VMEM(shape, jnp.bfloat16) for shape in shapes for _ in range(2)]


def child_update(where, front, cols, rows, x, lower):
    return pl.pallas_call(
        child_kernel,
        out_shape=(
            jax.ShapeDtypeStruct((STEPS * STEPS, TILE, TILE), jnp.float32),
            jax.ShapeDtypeStruct((front.shape[0], TILE), jnp.float32),
        ),
        in_specs=[SMEM] + [VMEM] * 5,
        out_specs=(VMEM, VMEM),
        scratch_shapes=panel_scratch(*front.shape),
        compiler_params=pltpu.CompilerParams(vmem_limit_bytes=58 << 20),
        name="child_update",
    )(where, front, cols, rows, x, lower)


def parent_kernel(where_ref, front_ref, cols_ref, own_ref, other_ref, x_ref, lower_ref, out_ref, factor_ref, *scratch):
    xs, cs, rs, ls, ts = (scratch[i : i + 2] for i in range(0, 10, 2))
    wide = 2 * TILE
    col, core = where_ref[0], where_ref[1]
    depth = own_ref.shape[1]
    for ref, which in ((own_ref, core), (other_ref, 1 - core)):
        for g in range(STEPS):
            at = pl.ds(pl.multiple_of(g * TILE + which * depth, depth), depth)
            rs[0][at, :], rs[1][at, :] = split(ref[g])
    solve_panels(col, cols_ref, x_ref, factor_ref, xs, cs, rs, ls, ts)

    @pl.when(core == 0)
    def _():
        factor_ref[:TILE, :] = lower_ref[...]

    left = (ls[0][...], ls[1][...])

    def chunk(n, carry):
        here = pl.ds(pl.multiple_of(n * wide, wide), wide)
        out_ref[:, here] = front_ref[:, here] - dot3(left, (ts[0][:, here], ts[1][:, here]), ((1,), (0,)))
        return carry

    lax.fori_loop(0, front_ref.shape[1] // wide, chunk, 0)
    out_ref[:, :TILE] = jnp.zeros((front_ref.shape[0], TILE), jnp.float32)

    @pl.when(core == 0)
    def _():
        out_ref[:TILE, :] = jnp.zeros((TILE, front_ref.shape[1]), jnp.float32)


def parent_update(where, front, cols, own, other, x, lower):
    return pl.pallas_call(
        parent_kernel,
        out_shape=(
            jax.ShapeDtypeStruct(front.shape, jnp.float32),
            jax.ShapeDtypeStruct((front.shape[0], TILE), jnp.float32),
        ),
        in_specs=[SMEM] + [VMEM] * 6,
        out_specs=(VMEM, VMEM),
        scratch_shapes=panel_scratch(*front.shape),
        compiler_params=pltpu.CompilerParams(vmem_limit_bytes=60 << 20),
        name="parent_update",
    )(where, front, cols, own, other, x, lower)


def assemble_kernel(rows_ref, cols_ref, front_ref, own_ref, other_ref, out_ref):
    tiles_row, tiles_col = (n // TILE for n in front_ref.shape)
    out_ref[...] = front_ref[...]
    for child in range(2):
        for i in range(tiles_row):
            source = rows_ref[child * tiles_row + i]

            def add(box_ref, base):
                at = slice(i * TILE, (i + 1) * TILE)
                for j in range(tiles_col):
                    place = cols_ref[child * tiles_col + j]

                    @pl.when(place >= 0)
                    def _():
                        out_ref[at, j * TILE : (j + 1) * TILE] += box_ref[base + place]

            @pl.when((source >= 0) & (source < STEPS * STEPS))
            def _():
                add(own_ref, source)

            @pl.when(source >= STEPS * STEPS)
            def _():
                add(other_ref, source - STEPS * STEPS)


def assemble(rows, cols, front, own, other):
    return pl.pallas_call(
        assemble_kernel,
        out_shape=jax.ShapeDtypeStruct(front.shape, jnp.float32),
        in_specs=[SMEM, SMEM] + [VMEM] * 3,
        out_specs=VMEM,
        compiler_params=pltpu.CompilerParams(vmem_limit_bytes=40 << 20),
        name="assemble",
    )(rows, cols, front, own, other)


def spread(x, axes):
    count = lax.axis_size(axes)
    copies = jnp.broadcast_to(x[None], (count,) + x.shape)
    return lax.all_to_all(copies, axes, 0, 0, tiled=True)


def after(x, first):
    return lax.optimization_barrier((x, first))[0]


def local(child_fronts, child_map, parent_front):
    child = lax.axis_index("sub")
    core = lax.axis_index("core")
    row = lax.axis_index(("y", "core"))
    col = lax.axis_index(COL)
    group = lax.axis_index(GROUP)
    front = child_fronts[0]
    kept = CBLK // STEPS - 1

    own = spread(spread(front[:TILE, :TILE], "y"), COL)
    other = lax.ppermute(own, "core", SWAP)
    columns = lax.all_gather(after(front[:, :TILE], other), COL, axis=0)
    rows = lax.all_gather(after(front[:TILE, :], other), ("y", "core"), axis=0, tiled=True)
    upper, inverse = factor(core, own, other)
    lower = lax.dynamic_slice(upper, (col * TILE, row * TILE), (TILE, TILE)).T
    mine = child_map[child] // (PBLK // STEPS)
    zero = jnp.zeros((1,), jnp.int32)
    where = jnp.concatenate(
        [
            col.reshape(1),
            lax.dynamic_slice(mine, (row * kept,), (kept,)),
            zero,
            lax.dynamic_slice(mine, (col * kept,), (kept,)),
        ]
    ).astype(jnp.int32)
    box, child_factor = child_update(where, front, columns, rows, inverse, lower)

    box = lax.all_to_all(box, GROUP + COL, 0, 0, tiled=True)
    box_other = lax.ppermute(box, "core", SWAP)
    tiles_row, tiles_col = parent_front.shape[0] // TILE, parent_front.shape[1] // TILE
    blocks = jnp.arange(PBLK, dtype=jnp.int32)
    number = jnp.arange(CBLK - STEPS, dtype=jnp.int32)
    source = jnp.max(jnp.where(child_map[:, :, None] == blocks, number[:, None], -1), axis=1)
    source_row = lax.dynamic_slice(source, (0, (2 * group + core) * tiles_row), (2, tiles_row))
    source_col = lax.dynamic_slice(source, (0, col * tiles_col), (2, tiles_col))
    whose = (source_row // kept % 2 != core).astype(jnp.int32) * (STEPS * STEPS)
    place = whose + jnp.arange(2, dtype=jnp.int32)[:, None] * (STEPS * STEPS // 2) + source_row // (2 * kept) * STEPS
    place_row = jnp.where(source_row >= 0, place, -1)
    place_col = jnp.where(source_col >= 0, source_col // kept, -1)
    front = assemble(place_row.reshape(-1), place_col.reshape(-1), parent_front, box, box_other)

    down = [(0, 1)]
    half = TILE // 2
    piece = jnp.where(core == 0, front[:half, :TILE], lax.ppermute(front[half:TILE, :TILE], "core", down))
    own = spread(spread(piece, GROUP), COL)
    other = lax.ppermute(own, "core", SWAP)
    columns = lax.all_gather(after(front[:, :TILE], other), COL, axis=0)
    strip = jnp.where(core == 0, front[:half, :], lax.ppermute(front[half:TILE, :], "core", down))
    rows_own = spread(after(strip, other), GROUP)
    rows_other = lax.ppermute(rows_own, "core", SWAP)
    upper, inverse = factor(core, own, other)
    lower = lax.dynamic_slice(upper, (col * TILE, group * TILE), (TILE, TILE)).T
    where = jnp.stack([col, core]).astype(jnp.int32)
    update, parent_factor = parent_update(where, front, columns, rows_own, rows_other, inverse, lower)
    return (child_factor[None], parent_factor, update)


def solution(mesh):
    shape = (2, 4, 2, 2, 4)
    fine = jax.sharding.Mesh(mesh.devices.reshape(shape), ("sub", "y", "core", "xlo", "z"))
    in_specs = (P("sub", ("y", "core"), COL), P(), P(("sub", "y", "core"), COL))
    out_specs = (P("sub", ("y", "core"), COL), P(("sub", "y", "core"), COL), P(("sub", "y", "core"), COL))
    return jax.shard_map(local, mesh=fine, in_specs=in_specs, out_specs=out_specs, check_vma=False)
```

time: 1420 us -> 499 us (0.35)
  other arithmetic: 577 us -> 3.39 us
  waiting for transfers between devices: 347 us -> 76.6 us
  local copies, waits for them, and re-layouts: 250 us -> 37 us
  matrix products: 199 us -> 0 us
  Pallas kernels: 0 us -> 195 us
  blocking collectives: 0 us -> 139 us
  starting transfers between devices: 9.6 us -> 29.2 us
    another operation x67 -> x1, other arithmetic: 514 us -> 0.61 us  [local(): where = jnp.stack([col, core]).astype(jnp.int32)]
    pallas_call x0 -> x5, Pallas kernels: none -> 195 us  [the longest x2 124 us: factor(): pl.pallas_call(factor_kernel, out_shape=(out, out), in_specs=[SMEM, VMEM,...]
    psum x1 -> x0, waiting for transfers between devices: 168 us -> none  [parent_gathered(): panel_rows, block = lax.psum((rows_piece, block_piece), ('sub', 'row'))]
    another operation x88 -> x0, matrix products: 164 us -> none  [the longest x60 115 us: solve_panel(): jax.scipy.linalg.solve_triangular(lower, jnp.swapaxes(panel, -1, -2), low...]
    all_to_all x0 -> x5, blocking collectives: none -> 139 us  [the longest x4 79.5 us: spread(): return lax.all_to_all(copies, axes, 0, 0, tiled=True)]
    gather x71 -> x0, local copies, waits for them, and re-layouts: 88.8 us -> none
    all_gather x4 -> x3, waiting for transfers between devices: 91.3 us -> 6.18 us  [the longest x1 6.18 us: local(): lax.all_gather(after(front[:TILE, :], other), ('y', 'core'), axis=0, tile...]
    another operation x100 -> x0, local copies, waits for them, and re-layouts: 60.6 us -> none
  transfers between devices with their start and end apart: 6 -> 10, of which waited for: 5 -> 6; matrix products, arithmetic and copies ran while one was open for 31% -> 5% of each run, Pallas kernels for 0% -> 25%
where the time goes in v1:
time: 499 us; the launch traced here: 495 us
  Pallas kernels  195 us (39%)
  blocking collectives  139 us (28%)
  waiting for transfers between devices  76.6 us (15%)
  local copies, waits for them, and re-layouts  37 us (7%)
  starting transfers between devices  29.2 us (6%)
  between operations  14.1 us (3%)
    pallas_call x2, Pallas kernels, factor(): pl.pallas_call(factor_kernel, out_shape=(out, out), in_specs=[SMEM, VMEM,...  124 us
    all_to_all x4, blocking collectives, spread(): return lax.all_to_all(copies, axes, 0, 0, tiled=True)  79.5 us
    all_to_all x1, blocking collectives, local(): box = lax.all_to_all(box, GROUP + COL, 0, 0, tiled=True)  59.8 us
    all_to_all x1, waiting for transfers between devices, spread(): return lax.all_to_all(copies, axes, 0, 0, tiled=True)  57.6 us
    pallas_call x1, Pallas kernels, parent_update(): pl.pallas_call(parent_kernel, out_shape=(jax.ShapeDtypeStruct(front.shape...  34.5 us
    pallas_call x1, Pallas kernels, child_update(): pl.pallas_call(child_kernel, out_shape=(jax.ShapeDtypeStruct((STEPS * STE...  30.8 us
    unnamed x16, local copies, waits for them, and re-layouts  13.1 us
    ppermute x1, starting transfers between devices, local(): rows_other = lax.ppermute(rows_own, 'core', SWAP)  12 us
  transfers between devices with their start and end apart: 10, of which 6 were waited for; matrix products, arithmetic and copies ran while one was open for 5% of the time, Pallas kernels for 25%

profile of v1, /device:TPU:1, one launch (start us, length us, event | category | flops | bytes accessed | tf_op | source)
XLA Modules:
  0.0 494.7 jit_solution(11066992064576076654)
XLA Ops:
  8.1 10.4 %all_to_all.30 = f32[4,128,128]{2,1,0:T(8,128)S(1)} all-to-all(f32[4,128,128]{2,1,0:T(8,128)S(1)} %broadcast_in_dim.28), channel_id=1, replica_groups=mesh['sub'=2,'y'=4,'core'=2,'xlo'=2,'z'=4] {'y'}, dimensions={0} | all-to-all | bytes 524288 | tf_op jit(solution)/shard_map/all_to_all | solution.py:292
  18.7 30.0 %all_to_all.31.own_ref = f32[8,4,128,128]{3,2,1,0:T(8,128)S(1)} all-to-all(f32[8,4,128,128]{3,2,1,0:T(8,128)S(1)} %broadcast_in_dim.29), channel_id=1, replica_groups=mesh['sub'=2,'y'=4,'core'=2,'xlo'=2,'z'=4] {'xlo','z'}, dimensions={0} | all-to-all | bytes 4194304 | tf_op jit(solution)/shard_map/all_to_all | solution.py:292
  48.7 3.8 collective-permute-start
  52.5 1.9 slice.36
  54.4 2.0 collective-permute-done.other_ref
  57.3 1.9 slice_bitcast_fusion
  59.3 62.7 %factor.2 = (f32[1024,1024]{1,0:T(8,128)S(1)}, f32[1024,1024]{1,0:T(8,128)S(1)}) custom-call(s32[1]{0:T(128)} %bitcast.6.core_ref, f32[8,4,128,128]{3,2,1,0:T(8,128)S(1)} %all_to_all.31.own_ref, f32[8,4,128,128]{3,2,1,0:T(8,128)} %collective-permute-done.other_ref), custom_call_target="tpu_custom_call" | custom-call | flops 99999997952 | bytes 16777216 | tf_op jit(solution)/shard_map/factor/pallas_call | solution.py:121
  122.0 2.0 copy-done.1
  124.0 2.0 copy-done.3
  126.0 5.5 %copy.8 = f32[1024,1024]{0,1:T(8,128)} copy(f32[1024,1024]{1,0:T(8,128)} %copy-done.3) | data formatting | bytes 8388608 | tf_op jit(solution)/shard_map/factor/pallas_call | solution.py:121
  132.9 6.2 %all-gather.6.cloned.1.call-done.rows_ref = f32[1024,1024]{1,0:T(8,128)} async-done(((f32[128,1024]{1,0:T(8,128)}), f32[1024,1024]{1,0:T(8,128)}) %all-gather.6.cloned.1.call-update) | async-done | bytes 4194320 | tf_op jit(solution)/shard_map/all_gather | solution.py:311
  139.1 30.8 %child_update.1 = (f32[64,128,128]{2,1,0:T(8,128)}, f32[1024,128]{1,0:T(8,128)}) custom-call(s32[16]{0:T(128)} %pad_add_fusion.where_ref, f32[1024,1024]{1,0:T(8,128)} %bitcast.18, f32[8,1024,128]{2,1,0:T(8,128)} %bitcast.19, f32[1024,1024]{1,0:T(8,128)} %all-gather.6.cloned.1.call-done.rows_ref, f32[1024,1024]{1,0:T(8,128)} %copy-done.1, ...), custom_call_target="tpu_custom_call" | custom-call | tf_op jit(solution)/shard_map/child_update/pallas_call | solution.py:194
  169.9 59.8 %all_to_all.32.own_ref = f32[64,128,128]{2,1,0:T(8,128)} all-to-all(f32[64,128,128]{2,1,0:T(8,128)} %get-tuple-element.20), channel_id=1, replica_groups=mesh['sub'=2,'y'=4,'core'=2,'xlo'=2,'z'=4] {'sub','y','xlo','z'}, dimensions={0} | all-to-all | bytes 8388608 | tf_op jit(solution)/shard_map/all_to_all | solution.py:326
  229.7 2.4 collective-permute-start.1
  232.5 6.7 %collective-permute-done.1.other_ref = f32[64,128,128]{2,1,0:T(8,128)} collective-permute-done((f32[64,128,128]{2,1,0:T(8,128)}, f32[64,128,128]{2,1,0:T(8,128)}, u32[]{:S(2)}, u32[]{:S(2)}) %collective-permute-start.1) | collective-permute-done | bytes 4194336 | tf_op jit(solution)/shard_map/ppermute | solution.py:327
  239.2 6.1 %assemble.1.front_ref = f32[768,1536]{1,0:T(8,128)S(1)} custom-call(s32[12]{0:T(128)S(1)} %reshape.43.rows_ref, s32[24]{0:T(128)S(1)} %reshape.44.cols_ref, f32[768,1536]{1,0:T(8,128)} %front_ref.1, f32[64,128,128]{2,1,0:T(8,128)} %all_to_all.32.own_ref, f32[64,128,128]{2,1,0:T(8,128)} %collective-permute-done.1.other_ref), custom_call_target="tpu_custom_call" | custom-call | tf_op jit(solution)/shard_map/assemble/pallas_call | solution.py:279
  245.3 2.1 copy-done
  248.8 1.8 collective-permute-done.2
  251.4 11.7 %all_to_all.33 = f32[8,64,128]{2,1,0:T(8,128)S(1)} all-to-all(f32[8,64,128]{2,1,0:T(8,128)S(1)} %broadcast_in_dim.33), channel_id=1, replica_groups=mesh['sub'=2,'y'=4,'core'=2,'xlo'=2,'z'=4] {'sub','y'}, dimensions={0} | all-to-all | bytes 524288 | tf_op jit(solution)/shard_map/all_to_all | solution.py:292
  263.3 27.4 %all_to_all.34.own_ref = f32[8,8,64,128]{3,2,1,0:T(8,128)S(1)} all-to-all(f32[8,8,64,128]{3,2,1,0:T(8,128)S(1)} %broadcast_in_dim.34), channel_id=1, replica_groups=mesh['sub'=2,'y'=4,'core'=2,'xlo'=2,'z'=4] {'xlo','z'}, dimensions={0} | all-to-all | bytes 4194304 | tf_op jit(solution)/shard_map/all_to_all | solution.py:292
  290.7 3.8 collective-permute-start.3
  296.9 2.3 collective-permute-done.4
  301.6 2.0 broadcast_in_dim.35
  303.6 4.4 all-to-all-start.5
  308.8 1.8 slice.38
  310.5 57.6 %all-to-all-done.5.own_ref = f32[8,64,1536]{2,1,0:T(8,128)} async-done(((f32[8,64,1536]{2,1,0:T(8,128)}), f32[8,64,1536]{2,1,0:T(8,128)}, u32[]{:S(2)}, u32[]{:S(2)}) %all-to-all-start.5) | async-done | bytes 3145760 | tf_op jit(solution)/shard_map/all_to_all | solution.py:292
  368.1 12.0 %collective-permute-start.5 = (f32[8,64,1536]{2,1,0:T(8,128)}, f32[8,64,1536]{2,1,0:T(8,128)}, u32[]{:S(2)}, u32[]{:S(2)}) collective-permute-start(f32[8,64,1536]{2,1,0:T(8,128)} %all-to-all-done.5.own_ref), channel_id=1, source_target_pairs={{0,8},{8,0},{1,9},{9,1},{2,10},{10,2},{3,11},{11,3},{4,12},{12,4},... | collective-permute-start | bytes 9437192 | tf_op jit(solution)/shard_map/ppermute | solution.py:348
  381.7 60.9 %factor.3 = (f32[1024,1024]{1,0:T(8,128)S(1)}, f32[1024,1024]{1,0:T(8,128)S(1)}) custom-call(s32[1]{0:T(128)} %bitcast.6.core_ref, f32[8,8,64,128]{3,2,1,0:T(8,128)S(1)} %all_to_all.34.own_ref, f32[8,8,64,128]{3,2,1,0:T(8,128)S(1)} %copy-done.6), custom_call_target="tpu_custom_call" | custom-call | flops 99999997952 | bytes 16777216 | tf_op jit(solution)/shard_map/factor/pallas_call | solution.py:121
  442.6 2.0 copy-done.2
  444.6 2.0 copy-done.4
  446.6 5.4 %copy.9 = f32[1024,1024]{0,1:T(8,128)} copy(f32[1024,1024]{1,0:T(8,128)} %copy-done.2) | data formatting | bytes 8388608 | tf_op jit(solution)/shard_map/factor/pallas_call | solution.py:121
  453.5 34.5 %parent_update.1 = (f32[768,1536]{1,0:T(8,128)}, f32[768,128]{1,0:T(8,128)}) custom-call(s32[2]{0:T(128)} %pad_add_fusion.1.where_ref, f32[768,1536]{1,0:T(8,128)} %copy-done, f32[8,768,128]{2,1,0:T(8,128)} %bitcast.20, f32[8,64,1536]{2,1,0:T(8,128)} %all-to-all-done.5.own_ref, f32[8,64,1536]{2,1,0:T(8,128)} %collective-permute-done.5.other_ref, ...), custom_call_target="tpu_custom_call" | custom-call | tf_op jit(solution)/shard_map/parent_update/pallas_call | solution.py:239
  (44 shorter events, 14.7 us)
Async XLA Ops:
  7.2 125.7 %all-gather.8.cloned.1.call-start = ((), (), s32[]{:S(2)}) async-start(), calls=%async_computation.7 | async-start | bytes 4718592 | tf_op jit(solution)/shard_map/all_gather | solution.py:310
  18.4 38.1 %copy-start.7 = (s32[2,56]{1,0:T(2,128)S(1)}, s32[2,56]{1,0:T(2,128)}, u32[]{:S(2)}) copy-start(s32[2,56]{1,0:T(2,128)} %param.4) | copy-start | bytes 1348
  48.7 7.8 %collective-permute-start = (f32[8,4,128,128]{3,2,1,0:T(8,128)S(1)}, f32[8,4,128,128]{3,2,1,0:T(8,128)}, u32[]{:S(2)}, u32[]{:S(2)}) collective-permute-start(f32[8,4,128,128]{3,2,1,0:T(8,128)S(1)} %all_to_all.31.own_ref), channel_id=1, source_target_pairs={{0,8},{8,0},{1,9},{9,1},{2,10},{10,2},{3,11},{11,3},{4,12},{12,4},... | collective-permute-start | bytes 6291464 | tf_op jit(solution)/shard_map/ppermute | solution.py:309
  56.5 82.6 %all-gather.6.cloned.1.call-start = ((), (), s32[]{:S(2)}) async-start(), calls=%async_computation.6 | async-start | bytes 4718592 | tf_op jit(solution)/shard_map/all_gather | solution.py:311
  122.0 2.0 copy-start.1
  124.0 2.0 copy-start.3
  229.7 9.5 %collective-permute-start.1 = (f32[64,128,128]{2,1,0:T(8,128)}, f32[64,128,128]{2,1,0:T(8,128)}, u32[]{:S(2)}, u32[]{:S(2)}) collective-permute-start(f32[64,128,128]{2,1,0:T(8,128)} %all_to_all.32.own_ref), channel_id=1, source_target_pairs={{0,8},{8,0},{1,9},{9,1},{2,10},{10,2},{3,11},{11,3},{4,12},{12,4},... | collective-permute-start | bytes 12582920 | tf_op jit(solution)/shard_map/ppermute | solution.py:327
  245.3 2.1 copy-start
  247.5 3.1 collective-permute-start.2
  290.7 9.5 %collective-permute-start.3 = (f32[8,8,64,128]{3,2,1,0:T(8,128)S(1)}, f32[8,8,64,128]{3,2,1,0:T(8,128)S(1)}, u32[]{:S(2)}, u32[]{:S(2)}) collective-permute-start(f32[8,8,64,128]{3,2,1,0:T(8,128)S(1)} %all_to_all.34.own_ref), channel_id=1, source_target_pairs={{0,8},{8,0},{1,9},{9,1},{2,10},{10,2},{3,11},{11,3},{4,12},{12,4},... | collective-permute-start | bytes 6291464 | tf_op jit(solution)/shard_map/ppermute | solution.py:344
  295.6 3.6 collective-permute-start.4
  300.2 1.3 copy-start.5
  303.6 64.5 %all-to-all-start.5 = ((f32[8,64,1536]{2,1,0:T(8,128)}), f32[8,64,1536]{2,1,0:T(8,128)}, u32[]{:S(2)}, u32[]{:S(2)}) async-start(f32[8,64,1536]{2,1,0:T(8,128)} %broadcast_in_dim.35), calls=%async_computation.5 | async-start | bytes 6291456 | tf_op jit(solution)/shard_map/all_to_all | solution.py:292
  308.1 145.4 %all-gather.10.cloned.1.call-start = ((), (), s32[]{:S(2)}) async-start(), calls=%async_computation.8 | async-start | bytes 3538944 | tf_op jit(solution)/shard_map/all_gather | solution.py:345
  368.1 85.4 %collective-permute-start.5 = (f32[8,64,1536]{2,1,0:T(8,128)}, f32[8,64,1536]{2,1,0:T(8,128)}, u32[]{:S(2)}, u32[]{:S(2)}) collective-permute-start(f32[8,64,1536]{2,1,0:T(8,128)} %all-to-all-done.5.own_ref), channel_id=1, source_target_pairs={{0,8},{8,0},{1,9},{9,1},{2,10},{10,2},{3,11},{11,3},{4,12},{12,4},... | collective-permute-start | bytes 9437192 | tf_op jit(solution)/shard_map/ppermute | solution.py:348
  380.1 1.6 copy-start.6
  442.6 2.0 copy-start.2
  444.6 2.0 copy-start.4
Sparse Core Ops, SparseCore 0:
  56.6 49.3 all-gather.7
  107.8 31.2 all-gather.5
  311.1 62.2 all-gather.9

commit v2 on v1

--- a/solution.py
+++ b/solution.py
@@ -32,57 +32,72 @@
     return dot(a[0], b[0]) + (dot(a[0], b[1]) + dot(a[1], b[0]))
 
 
-def factor_tile(s_ref, u_ref, x_ref):
+def factor_tile(s_ref, u_ref, x_ref, beside):
     full = (8, TILE)
+    count = TILE // 8
     lane = lax.broadcasted_iota(jnp.int32, full, 1)
     sub = lax.broadcasted_iota(jnp.int32, full, 0)
-    for p in range(TILE // 8):
+    s = [s_ref[8 * i : 8 * i + 8, :] for i in range(count)]
+    for p in range(count):
         j0 = 8 * p
         inside = (lane >= j0) & (lane < j0 + 8)
-        panel = s_ref[j0 : j0 + 8, :]
-        cols = [jnp.broadcast_to(panel[:, j0 + k : j0 + k + 1], full) for k in range(8)]
+        panel = s[p]
+        if p == 0:
+            cols = [jnp.broadcast_to(panel[:, j0 + k : j0 + k + 1], full) for k in range(8)]
         c = [[jnp.broadcast_to(cols[m][k : k + 1, :], full) if m >= k else None for m in range(8)] for k in range(8)]
-        low = [[None] * 8 for _ in range(8)]
-        inv, root = [None] * 8, [None] * 8
-        for k in range(8):
-            root[k] = lax.rsqrt(c[k][k])
-            inv[k] = root[k] * root[k]
-            for m in range(k + 1, 8):
-                low[m][k] = c[k][m] * inv[k]
-            for m in range(k + 1, 8):
-                for n in range(m, 8):
-                    c[m][n] = c[m][n] - low[m][k] * c[k][n]
         e = []
         for k in range(8):
             row = jnp.broadcast_to(panel[k : k + 1, :], full)
-            row = jnp.where(inside, jnp.where(lane == j0 + k, 1.0, 0.0), row)
-            for m in range(k):
-                row = row - low[k][m] * e[m]
-            e.append(row)
-        q = [None] * 8
-        for k in reversed(range(8)):
-            row = inv[k] * e[k]
+            e.append(jnp.where(inside, jnp.where(lane == j0 + k, 1.0, 0.0), row))
+        more = p + 1 < count
+        if more:
+            f = [jnp.broadcast_to(s[p + 1][:, j0 + k : j0 + k + 1], full) for k in range(8)]
+            later = jnp.where(inside, 0.0, s[p + 1])
+            cols = [jnp.broadcast_to(s[p + 1][:, j0 + 8 + k : j0 + 9 + k], full) for k in range(8)]
+        root = [None] * 8
+        for k in range(8):
+            root[k] = lax.rsqrt(c[k][k])
+            for m in range(k, 8):
+                c[k][m] = c[k][m] * root[k]
+            e[k] = e[k] * root[k]
+            if more:
+                f[k] = f[k] * root[k]
+                later = later - f[k] * e[k]
+                for n in range(8):
+                    cols[n] = cols[n] - f[k] * jnp.broadcast_to(f[k][n : n + 1, :], full)
             for m in range(k + 1, 8):
-                row = row - low[m][k] * q[m]
-            q[k] = row
+                for n in range(m, 8):
+                    c[m][n] = c[m][n] - c[k][m] * c[k][n]
+                e[m] = e[m] - c[k][m] * e[k]
+                if more:
+                    f[m] = f[m] - c[k][m] * f[k]
+        beside(p)
+        if p + 2 < count:
+            q = [None] * 8
+            for k in reversed(range(8)):
+                row = e[k]
+                for m in range(k + 1, 8):
+                    row = row - c[k][m] * q[m]
+                q[k] = row * root[k]
+            for i in range(p + 2, count):
+                new = jnp.where(inside, 0.0, s[i])
+                for k in range(8):
+                    new = new - jnp.broadcast_to(s[i][:, j0 + k : j0 + k + 1], full) * q[k]
+                s[i] = new
+        if more:
+            s[p + 1] = later
         out = jnp.zeros(full, jnp.float32)
         diag = jnp.zeros(full, jnp.float32)
         for k in range(8):
-            out = jnp.where(sub == k, e[k] * root[k], out)
+            out = jnp.where(sub == k, e[k], out)
             for m in range(k, 8):
-                diag = jnp.where((sub == k) & (lane == j0 + m), c[k][m] * root[k], diag)
+                diag = jnp.where((sub == k) & (lane == j0 + m), c[k][m], diag)
         x_ref[j0 : j0 + 8, :] = jnp.where(lane < j0 + 8, out, 0.0)
         u_ref[j0 : j0 + 8, :] = jnp.where(lane >= j0 + 8, out, diag)
-        for i in range(p + 1, TILE // 8):
-            old = s_ref[8 * i : 8 * i + 8, :]
-            new = jnp.where(inside, 0.0, old)
-            for k in range(8):
-                new = new - jnp.broadcast_to(old[:, j0 + k : j0 + k + 1], full) * q[k]
-            s_ref[8 * i : 8 * i + 8, :] = new
-
-
-def factor_kernel(core_ref, own_ref, other_ref, u_ref, x_ref, w_ref, s_ref, uk_ref, xk_ref, row_ref):
-    core = core_ref[0]
+
+
+def factor_kernel(where_ref, own_ref, other_ref, x_ref, lower_ref, w_ref, u_ref, d_ref, s_ref, xn_ref, xk_ref, last_ref, high_ref, rest_ref):
+    core, tile_row, tile_col = where_ref[0], where_ref[1], where_ref[2]
     groups, depth = own_ref.shape[1], own_ref.shape[2]
     pitch = ORDER // groups
     for ref, which in ((own_ref, core), (other_ref, 1 - core)):
@@ -92,44 +107,65 @@
                 w_ref[pl.ds(begin, depth), c * TILE : (c + 1) * TILE] = ref[c, g]
     block = lax.broadcasted_iota(jnp.int32, (TILE, ORDER), 1) // TILE
 
+    def place(k):
+        return pl.ds(pl.multiple_of(k * TILE, TILE), TILE)
+
+    def finish(k):
+        row = dot3(split(xk_ref[...]), split(w_ref[place(k), :]), ((1,), (0,)))
+        last_ref[...] = row
+        last_ref[:, place(k)] = xk_ref[...]
+        row = last_ref[...]
+        x_ref[place(k), :] = jnp.where(block <= k, row, 0.0)
+        u_ref[place(k), :] = jnp.where(block > k, row, 0.0)
+        high_ref[...], rest_ref[...] = split(row)
+
     def step(k, carry):
-        here = pl.ds(pl.multiple_of(k * TILE, TILE), TILE)
-        s_ref[...] = w_ref[here, here]
-        factor_tile(s_ref, uk_ref, xk_ref)
-        row_ref[...] = dot3(split(xk_ref[...]), split(w_ref[here, :]), ((1,), (0,)))
-        row_ref[:, here] = xk_ref[...]
-        new = row_ref[...]
-        x_ref[here, :] = jnp.where(block <= k, new, 0.0)
-        u_ref[here, :] = jnp.where(block > k, new, 0.0)
-        u_ref[here, here] = uk_ref[...]
-        right = split(new)
-
-        def trail(i, carry):
-            at = pl.ds(pl.multiple_of(i * TILE, TILE), TILE)
-            w_ref[at, here] = jnp.zeros((TILE, TILE), jnp.float32)
-            w_ref[at, :] -= dot3(split(row_ref[:, at].T), right, ((1,), (0,)))
-            return carry
-
-        lax.fori_loop(k + 1, STEPS, trail, 0)
+        before = k - 1
+
+        def beside(p):
+            if p == 0:
+                finish(jnp.maximum(before, 0))
+            elif p % 2 == 0:
+                i = p // 2
+                at = slice(i * TILE, (i + 1) * TILE)
+                mine = jnp.where(i > before, last_ref[:, at], 0.0).T
+                held = w_ref[at, :]
+                held = jnp.where((block == before) & (i > before), 0.0, held)
+                w_ref[at, :] = held - dot3(split(mine), (high_ref[...], rest_ref[...]), ((1,), (0,)))
+
+        factor_tile(s_ref, d_ref.at[place(k)], xn_ref, beside)
+        xk_ref[...] = xn_ref[...]
+        after_k = jnp.minimum(k + 1, STEPS - 1)
+        high, rest = split(dot3(split(xn_ref[...]), split(w_ref[place(k), place(after_k)]), ((1,), (0,))))
+        s_ref[...] = w_ref[place(after_k), place(after_k)] - dot3((high.T, rest.T), (high, rest), ((1,), (0,)))
         return carry
 
+    xk_ref[...] = jnp.zeros((TILE, TILE), jnp.float32)
+    s_ref[...] = w_ref[:TILE, :TILE]
     lax.fori_loop(0, STEPS, step, 0)
-
-
-def factor(core, own, other):
-    out = jax.ShapeDtypeStruct((ORDER, ORDER), jnp.float32)
+    finish(STEPS - 1)
+    tile = jnp.where(tile_row == tile_col, d_ref[place(tile_col), :], u_ref[place(tile_col), place(tile_row)])
+    lower_ref[...] = tile.T
+
+
+def factor(where, own, other):
     return pl.pallas_call(
         factor_kernel,
-        out_shape=(out, out),
+        out_shape=(
+            jax.ShapeDtypeStruct((ORDER, ORDER), jnp.float32),
+            jax.ShapeDtypeStruct((TILE, TILE), jnp.float32),
+        ),
         in_specs=[SMEM, VMEM, VMEM],
         out_specs=(VMEM, VMEM),
-        scratch_shapes=[pltpu.VMEM((ORDER, ORDER), jnp.float32)]
+        scratch_shapes=[pltpu.VMEM((ORDER, ORDER), jnp.float32)] * 2
+        + [pltpu.VMEM((ORDER, TILE), jnp.float32)]
         + [pltpu.VMEM((TILE, TILE), jnp.float32)] * 3
-        + [pltpu.VMEM((TILE, ORDER), jnp.float32)],
+        + [pltpu.VMEM((TILE, ORDER), jnp.float32)]
+        + [pltpu.VMEM((TILE, ORDER), jnp.bfloat16)] * 2,
         compiler_params=pltpu.CompilerParams(vmem_limit_bytes=40 << 20),
         cost_estimate=pl.CostEstimate(flops=100_000_000_000, bytes_accessed=16 << 20, transcendentals=0),
         name="factor",
-    )(core.reshape(1), own, other)
+    )(where, own, other)
 
 
 def solve_panels(col, cols_ref, x_ref, factor_ref, xs, cs, rs, ls, ts):
@@ -305,12 +341,12 @@
     front = child_fronts[0]
     kept = CBLK // STEPS - 1
 
-    own = spread(spread(front[:TILE, :TILE], "y"), COL)
+    first = spread(front[:TILE, :TILE], "y")
+    rows = lax.all_gather(after(front[:TILE, :], first), ("y", "core"), axis=0, tiled=True)
+    own = spread(first, COL)
     other = lax.ppermute(own, "core", SWAP)
-    columns = lax.all_gather(after(front[:, :TILE], other), COL, axis=0)
-    rows = lax.all_gather(after(front[:TILE, :], other), ("y", "core"), axis=0, tiled=True)
-    upper, inverse = factor(core, own, other)
-    lower = lax.dynamic_slice(upper, (col * TILE, row * TILE), (TILE, TILE)).T
+    columns = lax.all_gather(after(front[:, :TILE], own), COL, axis=0)
+    inverse, lower = factor(jnp.stack([core, row, col]).astype(jnp.int32), own, other)
     mine = child_map[child] // (PBLK // STEPS)
     zero = jnp.zeros((1,), jnp.int32)
     where = jnp.concatenate(
@@ -340,14 +376,15 @@
     down = [(0, 1)]
     half = TILE // 2
     piece = jnp.where(core == 0, front[:half, :TILE], lax.ppermute(front[half:TILE, :TILE], "core", down))
-    own = spread(spread(piece, GROUP), COL)
+    first = spread(piece, GROUP)
+    strip = jnp.where(core == 0, front[:half, :], lax.ppermute(front[half:TILE, :], "core", down))
+    rows_own = spread(after(strip, first), GROUP)
+    own = spread(first, COL)
     other = lax.ppermute(own, "core", SWAP)
-    columns = lax.all_gather(after(front[:, :TILE], other), COL, axis=0)
-    strip = jnp.where(core == 0, front[:half, :], lax.ppermute(front[half:TILE, :], "core", down))
-    rows_own = spread(after(strip, other), GROUP)
+    columns = lax.all_gather(after(front[:, :TILE], own), COL, axis=0)
+    inverse, lower = factor(jnp.stack([core, group, col]).astype(jnp.int32), own, other)
+    rows_own = after(rows_own, lower)
     rows_other = lax.ppermute(rows_own, "core", SWAP)
-    upper, inverse = factor(core, own, other)
-    lower = lax.dynamic_slice(upper, (col * TILE, group * TILE), (TILE, TILE)).T
     where = jnp.stack([col, core]).astype(jnp.int32)
     update, parent_factor = parent_update(where, front, columns, rows_own, rows_other, inverse, lower)
     return (child_factor[None], parent_factor, update)

time: 499 us -> 387 us (0.78)
  Pallas kernels: 195 us -> 145 us
  waiting for transfers between devices: 76.6 us -> 50.1 us
  local copies, waits for them, and re-layouts: 37 us -> 19.9 us
  blocking collectives: 139 us -> 127 us
    pallas_call x2, Pallas kernels: 124 us -> 73.3 us  [factor(): pl.pallas_call(factor_kernel, out_shape=(jax.ShapeDtypeStruct((ORDER, ORD...]
    all_to_all x1 -> x2, waiting for transfers between devices: 57.6 us -> 22.1 us  [spread(): return lax.all_to_all(copies, axes, 0, 0, tiled=True)]
    all_to_all x4 -> x3, blocking collectives: 79.5 us -> 68.5 us  [spread(): return lax.all_to_all(copies, axes, 0, 0, tiled=True)]
    pallas_call x2 -> x0, local copies, waits for them, and re-layouts: 10.9 us -> none  [factor(): pl.pallas_call(factor_kernel, out_shape=(out, out), in_specs=[SMEM, VMEM,...]
    ppermute x1, starting transfers between devices: 12 us -> 4.39 us  [local(): rows_other = lax.ppermute(rows_own, 'core', SWAP)]
    all_gather x3, waiting for transfers between devices: 6.18 us -> 12.5 us  [the longest x2 12.5 us: local(): columns = lax.all_gather(after(front[:, :TILE], own), COL, axis=0)]
    all_to_all x1 -> x2, starting transfers between devices: 4.45 us -> 9.47 us  [spread(): return lax.all_to_all(copies, axes, 0, 0, tiled=True)]
    unnamed x16 -> x14, local copies, waits for them, and re-layouts: 13.1 us -> 9.04 us
  transfers between devices with their start and end apart: 10 -> 11, of which waited for: 6 -> 8; matrix products, arithmetic and copies ran while one was open for 5% -> 3% of each run, Pallas kernels for 25% -> 19%
where the time goes in v2:
time: 387 us; the launch traced here: 386 us
  Pallas kernels  145 us (37%)
  blocking collectives  127 us (33%)
  waiting for transfers between devices  50.1 us (13%)
  starting transfers between devices  27.1 us (7%)
  local copies, waits for them, and re-layouts  19.9 us (5%)
  between operations  13.9 us (4%)
    pallas_call x2, Pallas kernels, factor(): pl.pallas_call(factor_kernel, out_shape=(jax.ShapeDtypeStruct((ORDER, ORD...  73.3 us
    all_to_all x3, blocking collectives, spread(): return lax.all_to_all(copies, axes, 0, 0, tiled=True)  68.5 us
    all_to_all x1, blocking collectives, local(): box = lax.all_to_all(box, GROUP + COL, 0, 0, tiled=True)  58.3 us
    pallas_call x1, Pallas kernels, parent_update(): pl.pallas_call(parent_kernel, out_shape=(jax.ShapeDtypeStruct(front.shape...  34.5 us
    pallas_call x1, Pallas kernels, child_update(): pl.pallas_call(child_kernel, out_shape=(jax.ShapeDtypeStruct((STEPS * STE...  30.7 us
    all_to_all x2, waiting for transfers between devices, spread(): return lax.all_to_all(copies, axes, 0, 0, tiled=True)  22.1 us
    all_gather x2, waiting for transfers between devices, local(): columns = lax.all_gather(after(front[:, :TILE], own), COL, axis=0)  12.5 us
    all_to_all x2, starting transfers between devices, spread(): return lax.all_to_all(copies, axes, 0, 0, tiled=True)  9.47 us
  transfers between devices with their start and end apart: 11, of which 8 were waited for; matrix products, arithmetic and copies ran while one was open for 3% of the time, Pallas kernels for 19%

profile of v2, /device:TPU:1, one launch (start us, length us, event | category | flops | bytes accessed | tf_op | source)
XLA Modules:
  0.0 386.4 jit_solution(11789619376765551290)
XLA Ops:
  8.7 5.0 %all-to-all-start = ((f32[4,128,128]{2,1,0:T(8,128)}), f32[4,128,128]{2,1,0:T(8,128)S(1)}, u32[]{:S(2)}, u32[]{:S(2)}) async-start(f32[4,128,128]{2,1,0:T(8,128)} %broadcast_in_dim.28), calls=%async_computation | async-start | bytes 524288 | tf_op jit(solution)/shard_map/all_to_all | solution.py:328
  13.7 1.9 slice_bitcast_fusion
  15.6 3.7 all-to-all-done
  19.6 30.0 %all_to_all.30.own_ref = f32[8,4,128,128]{3,2,1,0:T(8,128)S(1)} all-to-all(f32[8,4,128,128]{3,2,1,0:T(8,128)S(1)} %broadcast_in_dim.29), channel_id=1, replica_groups=mesh['sub'=2,'y'=4,'core'=2,'xlo'=2,'z'=4] {'xlo','z'}, dimensions={0} | all-to-all | bytes 4194304 | tf_op jit(solution)/shard_map/all_to_all | solution.py:328
  49.6 3.8 collective-permute-start
  53.5 1.9 slice.36
  56.2 1.2 collective-permute-done.other_ref
  57.4 36.7 %factor.2 = (f32[1024,1024]{1,0:T(8,128)S(1)}, f32[128,128]{1,0:T(8,128)S(1)}) custom-call(s32[3]{0:T(128)S(1)} %add_add_fusion.where_ref, f32[8,4,128,128]{3,2,1,0:T(8,128)S(1)} %all_to_all.30.own_ref, f32[8,4,128,128]{3,2,1,0:T(8,128)} %collective-permute-done.other_ref), custom_call_target="tpu_custom_call" | custom-call | flops 99999997952 | bytes 16777216 | tf_op jit(solution)/shard_map/factor/pallas_call | solution.py:152
  94.1 2.0 copy-done.1
  96.8 12.5 %all-gather.8.cloned.1.call-done = f32[8192,128]{1,0:T(8,128)} async-done(((f32[1024,128]{1,0:T(8,128)}), f32[8192,128]{1,0:T(8,128)}) %all-gather.8.cloned.1.call-update) | async-done | bytes 4194320 | tf_op jit(solution)/shard_map/all_gather | solution.py:348
  109.2 30.7 %child_update.1 = (f32[64,128,128]{2,1,0:T(8,128)}, f32[1024,128]{1,0:T(8,128)}) custom-call(s32[16]{0:T(128)} %pad_add_fusion.where_ref, f32[1024,1024]{1,0:T(8,128)} %bitcast.16, f32[8,1024,128]{2,1,0:T(8,128)} %bitcast.17, f32[1024,1024]{1,0:T(8,128)} %all-gather.6.cloned.1.call-done.rows_ref, f32[1024,1024]{1,0:T(8,128)} %copy-done.1, f32[128,128]{1,0:T(8,128)} %copy-done.4), custom_call_target="tpu_custom_call" | custom-call | tf_op jit(solution)/shard_map/child_update/pallas_call | solution.py:230
  140.0 58.3 %all_to_all.31.own_ref = f32[64,128,128]{2,1,0:T(8,128)} all-to-all(f32[64,128,128]{2,1,0:T(8,128)} %get-tuple-element.21), channel_id=1, replica_groups=mesh['sub'=2,'y'=4,'core'=2,'xlo'=2,'z'=4] {'sub','y','xlo','z'}, dimensions={0} | all-to-all | bytes 8388608 | tf_op jit(solution)/shard_map/all_to_all | solution.py:362
  198.3 2.8 collective-permute-start.1
  201.6 6.7 %collective-permute-done.1.other_ref = f32[64,128,128]{2,1,0:T(8,128)} collective-permute-done((f32[64,128,128]{2,1,0:T(8,128)}, f32[64,128,128]{2,1,0:T(8,128)}, u32[]{:S(2)}, u32[]{:S(2)}) %collective-permute-start.1) | collective-permute-done | bytes 4194336 | tf_op jit(solution)/shard_map/ppermute | solution.py:363
  208.2 6.4 %assemble.1.front_ref = f32[768,1536]{1,0:T(8,128)S(1)} custom-call(s32[12]{0:T(128)S(1)} %reshape.38.rows_ref, s32[24]{0:T(128)S(1)} %reshape.39.cols_ref, f32[768,1536]{1,0:T(8,128)} %front_ref.1, f32[64,128,128]{2,1,0:T(8,128)} %all_to_all.31.own_ref, f32[64,128,128]{2,1,0:T(8,128)} %collective-permute-done.1.other_ref), custom_call_target="tpu_custom_call" | custom-call | tf_op jit(solution)/shard_map/assemble/pallas_call | solution.py:315
  214.6 2.1 copy-done
  216.8 1.3 collective-permute-start.2
  218.0 1.8 collective-permute-done.2
  220.6 10.8 %all_to_all.32 = f32[8,64,128]{2,1,0:T(8,128)S(1)} all-to-all(f32[8,64,128]{2,1,0:T(8,128)S(1)} %broadcast_in_dim.33), channel_id=1, replica_groups=mesh['sub'=2,'y'=4,'core'=2,'xlo'=2,'z'=4] {'sub','y'}, dimensions={0} | all-to-all | bytes 524288 | tf_op jit(solution)/shard_map/all_to_all | solution.py:328
  231.7 27.7 %all_to_all.33.own_ref = f32[8,8,64,128]{3,2,1,0:T(8,128)S(1)} all-to-all(f32[8,8,64,128]{3,2,1,0:T(8,128)S(1)} %broadcast_in_dim.34), channel_id=1, replica_groups=mesh['sub'=2,'y'=4,'core'=2,'xlo'=2,'z'=4] {'xlo','z'}, dimensions={0} | all-to-all | bytes 4194304 | tf_op jit(solution)/shard_map/all_to_all | solution.py:328
  259.4 3.8 collective-permute-start.4
  264.2 1.3 collective-permute-start.3
  265.6 1.8 slice.38
  268.9 2.0 broadcast_in_dim.35
  270.9 4.5 %all-to-all-start.5 = ((f32[8,64,1536]{2,1,0:T(8,128)}), f32[8,64,1536]{2,1,0:T(8,128)}, u32[]{:S(2)}, u32[]{:S(2)}) async-start(f32[8,64,1536]{2,1,0:T(8,128)} %broadcast_in_dim.35), calls=%async_computation.5 | async-start | bytes 6291456 | tf_op jit(solution)/shard_map/all_to_all | solution.py:328
  276.2 36.6 %factor.3 = (f32[1024,1024]{1,0:T(8,128)S(1)}, f32[128,128]{1,0:T(8,128)S(1)}) custom-call(s32[3]{0:T(128)S(1)} %add_add_fusion.1.where_ref, f32[8,8,64,128]{3,2,1,0:T(8,128)S(1)} %all_to_all.33.own_ref, f32[8,8,64,128]{3,2,1,0:T(8,128)} %collective-permute-done.4.other_ref), custom_call_target="tpu_custom_call" | custom-call | flops 99999997952 | bytes 16777216 | tf_op jit(solution)/shard_map/factor/pallas_call | solution.py:152
  312.8 2.0 copy-done.2
  315.4 18.5 %all-to-all-done.5.own_ref = f32[8,64,1536]{2,1,0:T(8,128)} async-done(((f32[8,64,1536]{2,1,0:T(8,128)}), f32[8,64,1536]{2,1,0:T(8,128)}, u32[]{:S(2)}, u32[]{:S(2)}) %all-to-all-start.5) | async-done | bytes 3145760 | tf_op jit(solution)/shard_map/all_to_all | solution.py:328
  333.8 4.4 %collective-permute-start.5 = (f32[8,64,1536]{2,1,0:T(8,128)}, f32[8,64,1536]{2,1,0:T(8,128)S(1)}, u32[]{:S(2)}, u32[]{:S(2)}) collective-permute-start(f32[8,64,1536]{2,1,0:T(8,128)} %all-to-all-done.5.own_ref), channel_id=1, source_target_pairs={{0,8},{8,0},{1,9},{9,1},{2,10},{10,2},{3,11},{11,3},{4,12},{12,4},... | collective-permute-start | bytes 9437192 | tf_op jit(solution)/shard_map/ppermute | solution.py:387
  338.8 4.9 %collective-permute-done.5.other_ref = f32[8,64,1536]{2,1,0:T(8,128)S(1)} collective-permute-done((f32[8,64,1536]{2,1,0:T(8,128)}, f32[8,64,1536]{2,1,0:T(8,128)S(1)}, u32[]{:S(2)}, u32[]{:S(2)}) %collective-permute-start.5) | collective-permute-done | bytes 3145760 | tf_op jit(solution)/shard_map/ppermute | solution.py:387
  343.7 1.6 copy-done.5
  345.4 34.5 %parent_update.1 = (f32[768,1536]{1,0:T(8,128)}, f32[768,128]{1,0:T(8,128)}) custom-call(s32[2]{0:T(128)} %pad_add_fusion.1.where_ref, f32[768,1536]{1,0:T(8,128)} %copy-done, f32[8,768,128]{2,1,0:T(8,128)} %bitcast.18, f32[8,64,1536]{2,1,0:T(8,128)} %all-to-all-done.5.own_ref, f32[8,64,1536]{2,1,0:T(8,128)} %copy-done.5, f32[1024,1024]{1,0:T(8,128)} %copy-done.2, ...), custom_call_target="tpu_custom_call" | custom-call | tf_op jit(solution)/shard_map/parent_update/pallas_call | solution.py:275
  (41 shorter events, 9.4 us)
Async XLA Ops:
  8.7 10.6 %all-to-all-start = ((f32[4,128,128]{2,1,0:T(8,128)}), f32[4,128,128]{2,1,0:T(8,128)S(1)}, u32[]{:S(2)}, u32[]{:S(2)}) async-start(f32[4,128,128]{2,1,0:T(8,128)} %broadcast_in_dim.28), calls=%async_computation | async-start | bytes 524288 | tf_op jit(solution)/shard_map/all_to_all | solution.py:328
  13.7 83.0 %all-gather.6.cloned.1.call-start = ((), (), s32[]{:S(2)}) async-start(), calls=%async_computation.6 | async-start | bytes 4718592 | tf_op jit(solution)/shard_map/all_gather | solution.py:345
  15.6 39.7 %copy-start.6 = (s32[2,56]{1,0:T(2,128)S(1)}, s32[2,56]{1,0:T(2,128)}, u32[]{:S(2)}) copy-start(s32[2,56]{1,0:T(2,128)} %param.4) | copy-start | bytes 1348
  19.3 89.9 %all-gather.8.cloned.1.call-start = ((), (), s32[]{:S(2)}) async-start(), calls=%async_computation.7 | async-start | bytes 4718592 | tf_op jit(solution)/shard_map/all_gather | solution.py:348
  49.6 7.8 %collective-permute-start = (f32[8,4,128,128]{3,2,1,0:T(8,128)S(1)}, f32[8,4,128,128]{3,2,1,0:T(8,128)}, u32[]{:S(2)}, u32[]{:S(2)}) collective-permute-start(f32[8,4,128,128]{3,2,1,0:T(8,128)S(1)} %all_to_all.30.own_ref), channel_id=1, source_target_pairs={{0,8},{8,0},{1,9},{9,1},{2,10},{10,2},{3,11},{11,3},{4,12},{12,4},... | collective-permute-start | bytes 6291464 | tf_op jit(solution)/shard_map/ppermute | solution.py:347
  94.1 2.0 copy-start.1
  96.1 0.6 copy-start.4
  198.3 9.9 %collective-permute-start.1 = (f32[64,128,128]{2,1,0:T(8,128)}, f32[64,128,128]{2,1,0:T(8,128)}, u32[]{:S(2)}, u32[]{:S(2)}) collective-permute-start(f32[64,128,128]{2,1,0:T(8,128)} %all_to_all.31.own_ref), channel_id=1, source_target_pairs={{0,8},{8,0},{1,9},{9,1},{2,10},{10,2},{3,11},{11,3},{4,12},{12,4},... | collective-permute-start | bytes 12582920 | tf_op jit(solution)/shard_map/ppermute | solution.py:363
  214.6 2.2 copy-start
  216.8 3.1 collective-permute-start.2
  259.4 16.7 %collective-permute-start.4 = (f32[8,8,64,128]{3,2,1,0:T(8,128)S(1)}, f32[8,8,64,128]{3,2,1,0:T(8,128)}, u32[]{:S(2)}, u32[]{:S(2)}) collective-permute-start(f32[8,8,64,128]{3,2,1,0:T(8,128)S(1)} %all_to_all.33.own_ref), channel_id=1, source_target_pairs={{0,8},{8,0},{1,9},{9,1},{2,10},{10,2},{3,11},{11,3},{4,12},{12,4},... | collective-permute-start | bytes 6291464 | tf_op jit(solution)/shard_map/ppermute | solution.py:383
  264.2 3.6 collective-permute-start.3
  270.9 62.9 %all-to-all-start.5 = ((f32[8,64,1536]{2,1,0:T(8,128)}), f32[8,64,1536]{2,1,0:T(8,128)}, u32[]{:S(2)}, u32[]{:S(2)}) async-start(f32[8,64,1536]{2,1,0:T(8,128)} %broadcast_in_dim.35), calls=%async_computation.5 | async-start | bytes 6291456 | tf_op jit(solution)/shard_map/all_to_all | solution.py:328
  275.4 68.3 %all-gather.10.cloned.1.call-start = ((), (), s32[]{:S(2)}) async-start(), calls=%async_computation.8 | async-start | bytes 3538944 | tf_op jit(solution)/shard_map/all_gather | solution.py:384
  312.7 2.0 copy-start.2
  314.7 0.6 copy-start.3
  333.8 9.9 %collective-permute-start.5 = (f32[8,64,1536]{2,1,0:T(8,128)}, f32[8,64,1536]{2,1,0:T(8,128)S(1)}, u32[]{:S(2)}, u32[]{:S(2)}) collective-permute-start(f32[8,64,1536]{2,1,0:T(8,128)} %all-to-all-done.5.own_ref), channel_id=1, source_target_pairs={{0,8},{8,0},{1,9},{9,1},{2,10},{10,2},{3,11},{11,3},{4,12},{12,4},... | collective-permute-start | bytes 9437192 | tf_op jit(solution)/shard_map/ppermute | solution.py:387
  343.7 1.7 copy-start.5
Sparse Core Ops, SparseCore 0:
  19.4 34.2 all-gather.5
  56.3 52.8 all-gather.7
  278.5 62.2 all-gather.9
